TPU v7x, 32 devices: a whole 2x2x4 slice. The times are simulated.
32 devices in a mesh: grp: 2 (over y), blk: 4 (over z), head: 4 (over x, core).
Axes of the slice: x: 2, y: 2, z: 4, core: 2. Of those that a mesh axis runs over, the one named last changes fastest.
Arguments:
- queries: bfloat16 [256, 16384], P(('grp', 'blk'), 'head'), parts along dimension 0, may hold values from -80 to 80
- kv_cache: bfloat16 [64, 512, 8, 256], P(('grp', 'blk'), None, 'head'), parts along dimension 0, may hold values from -4 to 4
- draft_kv: bfloat16 [64, 4, 8, 256], P(('grp', 'blk'), None, 'head'), parts along dimension 0, may hold values from -5 to 5
- cache_len: int32 [64], P(('grp', 'blk')), parts along dimension 0, may hold values from 2 to 512, as said below
- accepted: int32 [64, 4], P(('grp', 'blk')), parts along dimension 0, may hold values from 0 to 1, as said below
- w_out: bfloat16 [16384, 16384], P('head', 'blk'), may hold values from -0.046875 to 0.046875
- residual: bfloat16 [256, 16384], P(('grp', 'head'), 'blk'), parts along dimension 0, may hold values from -12 to 12
- norm_gain: bfloat16 [16384], P('blk'), may hold values from 0.5 to 1.5
Outputs:
- residual_out: bfloat16 [256, 16384], P(('grp', 'head'), 'blk'), parts along dimension 0
- normed: bfloat16 [256, 16384], P(('grp', 'head'), 'blk'), parts along dimension 0
There are 2 independent parts, one for each index of `grp`. A program takes and returns all parts, laid end to end along the dimension named above; an argument that names none is the same for every part. Nothing has to cross between parts.
Inputs may be any that keep to these rules, and one draw needn't show every extreme that they name: `cache_len`: every sequence has at least two live slots; in every draw some sequences of every index of blk use all 512 slots. `accepted`: each row holds ones followed by zeros.
All inputs are finite; a program needn't handle non-finite values.
Results may differ from a plain program's by a relative error of at most 0.0038.
Values may be sent and summed in bfloat16 or wider, within the bound.
A program may use at most 128 MiB of HBM per device.

v0:
```python
import jax
import jax.numpy as jnp
from jax import lax
from jax.sharding import PartitionSpec as P


def attend_local(query_rows, cache_rows, draft_rows, length, accept_row):
    head_dim = cache_rows.shape[-1] // 2
    scaling = head_dim ** (-0.5)
    cache_keys = cache_rows[..., :head_dim]
    cache_values = cache_rows[..., head_dim:]
    draft_keys = draft_rows[..., :head_dim]
    draft_values = draft_rows[..., head_dim:]
    cache_scores = (
        jnp.einsum("jkgd,pkd->kjgp", query_rows, cache_keys, preferred_element_type=jnp.float32)
        * scaling
    )
    draft_scores = (
        jnp.einsum("jkgd,ikd->kjgi", query_rows, draft_keys, preferred_element_type=jnp.float32)
        * scaling
    )
    slots = jnp.arange(cache_rows.shape[0], dtype=jnp.int32)
    cache_scores = jnp.where(slots < length, cache_scores, -1e30)
    draft_len = draft_rows.shape[0]
    later = jnp.arange(draft_len, dtype=jnp.int32)[:, None]
    earlier = jnp.arange(draft_len, dtype=jnp.int32)[None, :]
    visible = (earlier == later) | (earlier < later) & (accept_row[None, :] == 1)
    draft_scores = jnp.where(visible[None, :, None, :], draft_scores, -1e30)
    top_score = jnp.maximum(jnp.max(cache_scores, axis=-1), jnp.max(draft_scores, axis=-1))[
        ..., None
    ]
    cache_exp = jnp.exp(cache_scores - top_score)
    draft_exp = jnp.exp(draft_scores - top_score)
    totals = jnp.sum(cache_exp, axis=-1, keepdims=True) + jnp.sum(draft_exp, axis=-1, keepdims=True)
    cache_probs = (cache_exp / totals).astype(jnp.bfloat16)
    draft_probs = (draft_exp / totals).astype(jnp.bfloat16)
    context = jnp.einsum(
        "kjgp,pkd->jkgd", cache_probs, cache_values, preferred_element_type=jnp.float32
    )
    context = context + jnp.einsum(
        "kjgi,ikd->jkgd", draft_probs, draft_values, preferred_element_type=jnp.float32
    )
    return context.astype(jnp.bfloat16).reshape(draft_len, -1)


def local(queries, kv_cache, draft_kv, cache_len, accepted, w_out, residual, norm_gain):
    seq_count = kv_cache.shape[0]
    kv_local = kv_cache.shape[2]
    head_dim = kv_cache.shape[3] // 2
    draft_len = draft_kv.shape[1]
    group_size = queries.shape[1] // (kv_local * head_dim)
    query_rows = queries.reshape(seq_count, draft_len, kv_local, group_size, head_dim)
    context = jax.vmap(attend_local)(query_rows, kv_cache, draft_kv, cache_len, accepted)
    context = context.reshape(seq_count * draft_len, -1)
    partial_terms = jnp.dot(
        lax.all_gather(context, "blk", axis=0, tiled=True),
        w_out,
        preferred_element_type=jnp.float32,
    )
    attended = lax.psum_scatter(partial_terms, "head", scatter_dimension=0, tiled=True)
    summed = residual.astype(jnp.float32) + attended
    squares = lax.psum(jnp.sum(summed * summed, axis=1), "blk")
    full_width = summed.shape[1] * lax.axis_size("blk")
    inverse_rms = lax.rsqrt(squares / full_width + 1e-05)
    normed = summed * inverse_rms[:, None] * norm_gain.astype(jnp.float32)[None, :]
    return (summed.astype(jnp.bfloat16), normed.astype(jnp.bfloat16))


def solution(mesh):
    return jax.shard_map(
        local,
        mesh=mesh,
        in_specs=(
            P(("grp", "blk"), "head"),
            P(("grp", "blk"), None, "head", None),
            P(("grp", "blk"), None, "head", None),
            P(("grp", "blk")),
            P(("grp", "blk"), None),
            P("head", "blk"),
            P(("grp", "head"), "blk"),
            P("blk"),
        ),
        out_specs=(P(("grp", "head"), "blk"), P(("grp", "head"), "blk")),
        check_vma=False,
    )
```

profile of v0, /device:TPU:0, one launch (start us, length us, event | category | flops | bytes accessed | tf_op | source)
XLA Modules:
  0.0 118.9 jit_solution(2009683724311233143)
XLA Ops:
  7.2 0.0 all-gather.2.cloned.1.call-start
  7.2 0.7 iota_compare_fusion
  8.0 5.7 %fusion.22 = (bf16[8,512,2,128]{3,2,1,0:T(2,128)(2,1)}, bf16[8,512,2,128]{3,2,1,0:T(2,128)(2,1)S(1)}) fusion(bf16[8,512,2,256]{3,2,1,0:T(2,128)(2,1)} %param.9), kind=kLoop, calls=%fused_computation.41 | loop fusion | bytes 8388608 | tf_op jit(solution)/shard_map/vmap()/slice | solution.py:11
  13.7 0.0 copy-done.2
  13.8 0.1 copy.19
  13.9 0.0 copy-done.3
  13.9 0.9 fusion.2
  14.9 0.8 fusion.24
  15.6 0.7 fusion.3
  16.3 0.1 fusion.16
  16.5 0.3 fusion.17
  16.8 0.0 copy-done
  16.8 0.9 fusion.6
  17.8 0.8 reshape.53
  18.6 0.0 all-gather.2.cloned.1.call-update
  18.6 0.0 reduce-scatter.2.cloned.1.call-start
  18.6 30.7 %all-gather.2.cloned.1.call-done = bf16[128,4096]{1,0:T(8,128)(2,1)} async-done(((bf16[32,4096]{1,0:T(8,128)(2,1)}), bf16[128,4096]{1,0:T(8,128)(2,1)}) %all-gather.2.cloned.1.call-update) | async-done | bytes 1048592 | tf_op jit(solution)/shard_map/all_gather | solution.py:56
  49.4 16.7 %fusion.25 = f32[128,4096]{1,0:T(8,128)} fusion(bf16[128,4096]{1,0:T(8,128)(2,1)} %all-gather.2.cloned.1.call-done, bf16[4096,4096]{1,0:T(8,128)(2,1)} %param.13), kind=kOutput, calls=%fused_computation.44 | convolution fusion | flops 4294967296 | bytes 36700160 | tf_op jit(solution)/shard_map/dot_general | solution.py:55
  66.1 0.0 reduce-scatter.2.cloned.1.call-update
  66.1 0.7 copy-done.4
  66.8 30.4 %reduce-scatter.2.cloned.1.call-done = f32[32,4096]{1,0:T(8,128)} async-done(((f32[128,4096]{1,0:T(8,128)}), f32[32,4096]{1,0:T(8,128)}) %reduce-scatter.2.cloned.1.call-update) | async-done | bytes 524304 | tf_op jit(solution)/shard_map/reduce_scatter | solution.py:60
  97.2 1.2 %multiply_reduce_fusion = f32[32]{0:T(128)S(1)} fusion(f32[32,4096]{1,0:T(8,128)} %reduce-scatter.2.cloned.1.call-done, bf16[32,4096]{1,0:T(8,128)(2,1)S(1)} %copy-done.1), kind=kLoop, calls=%fused_computation.20 | loop fusion | flops 524256 | bytes 786560 | tf_op jit(solution)/shard_map/reduce_sum | solution.py:62
  98.4 11.7 %psum.7 = f32[32]{0:T(128)S(1)} all-reduce(f32[32]{0:T(128)S(1)} %multiply_reduce_fusion), channel_id=1, replica_groups=mesh['grp'=2,'blk'=4,'head'=4] {'blk'}, use_global_device_ids=true, to_apply=%region_6.7 | all-reduce | flops 32 | bytes 256 | tf_op jit(solution)/shard_map/psum | solution.py:62
  110.1 1.9 %multiply_convert_fusion = (bf16[32,4096]{1,0:T(8,128)(2,1)}, bf16[32,4096]{1,0:T(8,128)(2,1)}) fusion(f32[4096]{0:T(1024)S(1)} %convert_element_type.30, f32[32]{0:T(128)S(1)} %add_rsqrt_fusion, f32[32,4096]{1,0:T(8,128)} %reduce-scatter.2.cloned.1.call-done, bf16[32,4096]{1,0:T(8,128)(2,1)S(1)} %copy-done.1), kind=kLoop, calls=%fused_computation.19 | loop fusion | flops 786432 | bytes 1327232 | tf_op jit(solution)/shard_map/convert_element_type | solution.py:66
  (18 shorter events, 0.2 us)
Async XLA Ops:
  7.2 42.2 %all-gather.2.cloned.1.call-start = ((), (), s32[]{:S(2)}) async-start(), calls=%async_computation.1 | async-start | bytes 1310720 | tf_op jit(solution)/shard_map/all_gather | solution.py:56
  8.0 5.7 %copy-start.2 = (bf16[32,4096]{1,0:T(8,128)(2,1)S(1)}, bf16[32,4096]{1,0:T(8,128)(2,1)}, u32[]{:S(2)}) copy-start(bf16[32,4096]{1,0:T(8,128)(2,1)} %param.8) | copy-start | bytes 786436
  8.0 5.8 %copy-start.5 = (s32[8,4]{0,1:T(4,128)S(1)}, s32[8,4]{0,1:T(4,128)}, u32[]{:S(2)}) copy-start(s32[8,4]{0,1:T(4,128)} %param.12) | copy-start | bytes 388
  8.0 5.9 %copy-start.3 = (bf16[8,4,2,256]{3,2,1,0:T(2,128)(2,1)S(1)}, bf16[8,4,2,256]{3,2,1,0:T(2,128)(2,1)}, u32[]{:S(2)}) copy-start(bf16[8,4,2,256]{3,2,1,0:T(2,128)(2,1)} %param.10) | copy-start | bytes 98308
  14.9 1.9 %copy-start = (bf16[8,512,2,128]{3,2,1,0:T(2,128)(2,1)S(1)}, bf16[8,512,2,128]{3,2,1,0:T(2,128)(2,1)}, u32[]{:S(2)}) copy-start(bf16[8,512,2,128]{3,2,1,0:T(2,128)(2,1)} %get-tuple-element.2) | copy-start | bytes 6291460
  18.6 78.6 %reduce-scatter.2.cloned.1.call-start = ((), (), s32[]{:S(2)}) async-start(), calls=%async_computation.2 | async-start | bytes 2621440 | tf_op jit(solution)/shard_map/reduce_scatter | solution.py:60
  66.1 0.7 copy-start.4
  66.1 31.1 %copy-start.1 = (bf16[32,4096]{1,0:T(8,128)(2,1)S(1)}, bf16[32,4096]{1,0:T(8,128)(2,1)}, u32[]{:S(2)}) copy-start(bf16[32,4096]{1,0:T(8,128)(2,1)} %param.14) | copy-start | bytes 786436
Sparse Core Ops, SparseCore 0:
  18.7 30.6 all-gather.1
  66.3 30.9 reduce-scatter.1
where the time goes:
time: 119 us
  waiting for transfers between devices  61.2 us (51%)
  matrix products  19.6 us (16%)
  between operations  14.1 us (12%)
  blocking collectives  11.7 us (10%)
  local copies, waits for them, and re-layouts  7.41 us (6%)
  other arithmetic  4.73 us (4%)
    all_gather x1, waiting for transfers between devices, local(): lax.all_gather(context, 'blk', axis=0, tiled=True)  30.7 us
    reduce_scatter x1, waiting for transfers between devices, local(): lax.psum_scatter(partial_terms, 'head', scatter_dimension=0, tiled=True)  30.4 us
    dot_general x1, matrix products, local(): jnp.dot(lax.all_gather(context, 'blk', axis=0, tiled=True), w_out, prefer...  16.7 us
    psum x1, blocking collectives, local(): squares = lax.psum(jnp.sum(summed * summed, axis=1), 'blk')  11.7 us
    slice x1, local copies, waits for them, and re-layouts, attend_local(): cache_values = cache_rows[..., head_dim:]  5.72 us
  transfers between devices with their start and end apart: 2, of which 2 were waited for; matrix products, arithmetic and copies ran while one was open for 0% of the time, Pallas kernels for 0%

commit v1 on v0

--- a/solution.py
+++ b/solution.py
@@ -1,7 +1,15 @@
+import functools
+
 import jax
 import jax.numpy as jnp
 from jax import lax
+from jax.experimental import pallas as pl
+from jax.experimental.pallas import tpu as pltpu
 from jax.sharding import PartitionSpec as P
+
+MESH = pl.DeviceIdType.MESH
+CHUNKS = 4
+TILE = 512
 
 
 def attend_local(query_rows, cache_rows, draft_rows, length, accept_row):
@@ -43,7 +51,312 @@
     return context.astype(jnp.bfloat16).reshape(draft_len, -1)
 
 
-def local(queries, kv_cache, draft_kv, cache_len, accepted, w_out, residual, norm_gain):
+def project_kernel(
+    blocks, heads,
+    ctx_ref, w_ref, res_ref, gain_ref, out_ref, norm_ref,
+    gat, wv, acc, send_a, recv_a, send_b, recv_b, squares,
+    w_sem, up_s, up_r, dn_s, dn_r, a_s, a_r, b_s, b_r, q_s, q_r,
+):
+    rows, depth = ctx_ref.shape
+    wide = w_ref.shape[1]
+    own_rows = res_ref.shape[0]
+    kc = depth // CHUNKS
+    nt = min(TILE, wide)
+    tiles = wide // nt
+    pairs = heads // 2
+    blk = lax.axis_index("blk")
+    head = lax.axis_index("head")
+    side = lax.rem(head, 2)
+    chip = head // 2
+    partner = chip * 2 + (1 - side)
+    full = wide * blocks
+
+    def w_copy(c):
+        part = pl.ds(c * kc, kc)
+        return pltpu.make_async_copy(w_ref.at[part], wv.at[part], w_sem.at[c])
+
+    def up_copy(t, c, src=None):
+        block = lax.rem(blk - t + blocks, blocks)
+        cols = pl.ds(pl.multiple_of(c * kc, kc), kc)
+        src = gat.at[block, :, cols] if src is None else src.at[:, cols]
+        n = t * CHUNKS + c
+        return pltpu.make_async_remote_copy(
+            src, gat.at[block, :, cols], up_s.at[n], up_r.at[n],
+            device_id={"blk": lax.rem(blk + 1, blocks)}, device_id_type=MESH)
+
+    def dn_copy(t, c, src=None):
+        block = lax.rem(blk + t, blocks)
+        cols = pl.ds(pl.multiple_of(c * kc, kc), kc)
+        src = gat.at[block, :, cols] if src is None else src.at[:, cols]
+        n = t * CHUNKS + c
+        return pltpu.make_async_remote_copy(
+            src, gat.at[block, :, cols], dn_s.at[n], dn_r.at[n],
+            device_id={"blk": lax.rem(blk + blocks - 1, blocks)}, device_id_type=MESH)
+
+    def up_wait(t, c):
+        block = lax.rem(blk - 1 - t + blocks, blocks)
+        cols = pl.ds(pl.multiple_of(c * kc, kc), kc)
+        n = t * CHUNKS + c
+        pltpu.make_async_remote_copy(
+            gat.at[block, :, cols], gat.at[block, :, cols], up_s.at[n], up_r.at[n],
+            device_id={"blk": lax.rem(blk + 1, blocks)}, device_id_type=MESH).wait_recv()
+
+    def dn_wait(t, c):
+        block = lax.rem(blk + 1 + t, blocks)
+        cols = pl.ds(pl.multiple_of(c * kc, kc), kc)
+        n = t * CHUNKS + c
+        pltpu.make_async_remote_copy(
+            gat.at[block, :, cols], gat.at[block, :, cols], dn_s.at[n], dn_r.at[n],
+            device_id={"blk": lax.rem(blk + 1, blocks)}, device_id_type=MESH).wait_recv()
+
+    for c in range(CHUNKS):
+        w_copy(c).start()
+
+    barrier = pltpu.get_barrier_semaphore()
+    for k in range(1, blocks):
+        pl.semaphore_signal(barrier, inc=1, device_id={"blk": lax.rem(blk + k, blocks)},
+                            device_id_type=MESH)
+    pl.semaphore_signal(barrier, inc=1, device_id={"head": partner}, device_id_type=MESH)
+    for k in range(1, pairs):
+        pl.semaphore_signal(
+            barrier, inc=1,
+            device_id={"head": lax.rem(chip + k, pairs) * 2 + side}, device_id_type=MESH)
+    pl.semaphore_wait(barrier, blocks - 1 + 1 + pairs - 1)
+
+    for c in range(CHUNKS):
+        @pl.when(blk + 1 < blocks)
+        def _():
+            up_copy(0, c, ctx_ref).start()
+
+        @pl.when(blk > 0)
+        def _():
+            dn_copy(0, c, ctx_ref).start()
+
+    gat[pl.ds(blk, 1)] = ctx_ref[...][None]
+
+    inner = jnp.logical_and(blk > 0, blk + 1 < blocks)
+
+    def forward(n, carry):
+        t = n // CHUNKS
+        c = lax.rem(n, CHUNKS)
+
+        @pl.when(jnp.logical_and(inner, blk - 1 - t >= 0))
+        def _():
+            up_wait(t, c)
+            up_copy(t + 1, c).start()
+
+        @pl.when(jnp.logical_and(inner, blk + 1 + t < blocks))
+        def _():
+            dn_wait(t, c)
+            dn_copy(t + 1, c).start()
+
+        return carry
+
+    lax.fori_loop(0, (blocks - 2) * CHUNKS, forward, 0)
+
+    def arrived(c):
+        w_copy(c).wait()
+
+        def one(t, carry):
+            @pl.when(blk == blocks - 1)
+            def _():
+                up_wait(t, c)
+
+            @pl.when(blk == 0)
+            def _():
+                dn_wait(t, c)
+
+            return carry
+
+        lax.fori_loop(0, blocks - 1, one, 0)
+
+    def product(c, n):
+        x = gat[:, :, c * kc:(c + 1) * kc].reshape(blocks * rows, kc)
+        return jnp.dot(x, wv[c * kc:(c + 1) * kc, n], preferred_element_type=jnp.float32)
+
+    for c in range(CHUNKS - 1):
+        arrived(c)
+
+        def tile_of(j, carry):
+            n = pl.ds(pl.multiple_of(j * nt, nt), nt)
+            if c == 0:
+                acc[:, n] = product(c, n)
+            else:
+                acc[:, n] = acc[:, n] + product(c, n)
+            return carry
+
+        lax.fori_loop(0, tiles, tile_of, 0)
+
+    arrived(CHUNKS - 1)
+
+    def a_copy(j):
+        return pltpu.make_async_remote_copy(
+            send_a.at[j], recv_a.at[j], a_s.at[j], a_r.at[j],
+            device_id={"head": partner}, device_id_type=MESH)
+
+    def b_copy(j, k):
+        to = lax.rem(chip + k, pairs)
+        n = j * (pairs - 1) + k - 1
+        return pltpu.make_async_remote_copy(
+            send_b.at[n], recv_b.at[n], b_s.at[n], b_r.at[n],
+            device_id={"head": to * 2 + side}, device_id_type=MESH)
+
+    def pair_sum(j):
+        n = pl.ds(pl.multiple_of(j * nt, nt), nt)
+        a_copy(j).wait_recv()
+        for k in range(pairs):
+            to = lax.rem(chip + k, pairs)
+            at = pl.ds(pl.multiple_of((to * 2 + side) * own_rows, own_rows), own_rows)
+            total = acc[at, n] + recv_a[j, to].astype(jnp.float32)
+            if k == 0:
+                acc[at, n] = total
+            else:
+                send_b[j * (pairs - 1) + k - 1] = total.astype(jnp.bfloat16)
+                b_copy(j, k).start()
+
+    def last(j, carry):
+        n = pl.ds(pl.multiple_of(j * nt, nt), nt)
+        acc[:, n] = acc[:, n] + product(CHUNKS - 1, n)
+        for x in range(pairs):
+            at = pl.ds(pl.multiple_of((x * 2 + 1 - side) * own_rows, own_rows), own_rows)
+            send_a[j, x] = acc[at, n].astype(jnp.bfloat16)
+        a_copy(j).start()
+
+        @pl.when(j > 0)
+        def _():
+            pair_sum(j - 1)
+
+        return carry
+
+    lax.fori_loop(0, tiles, last, 0)
+    pair_sum(tiles - 1)
+
+    squares[blk] = jnp.zeros((own_rows, 128), jnp.float32)
+    mine = pl.ds(pl.multiple_of(head * own_rows, own_rows), own_rows)
+
+    def finish(j, carry):
+        n = pl.ds(pl.multiple_of(j * nt, nt), nt)
+        total = acc[mine, n]
+        for k in range(1, pairs):
+            b_copy(j, k).wait_recv()
+            total = total + recv_b[j * (pairs - 1) + k - 1].astype(jnp.float32)
+        total = total + res_ref[:, n].astype(jnp.float32)
+        acc[mine, n] = total
+        out_ref[:, n] = total.astype(jnp.bfloat16)
+        power = total * total
+        part = power[:, 0:128]
+        for v in range(1, nt // 128):
+            part = part + power[:, v * 128:(v + 1) * 128]
+        squares[blk] = squares[blk] + part
+        return carry
+
+    lax.fori_loop(0, tiles, finish, 0)
+
+    def q_copy(k):
+        return pltpu.make_async_remote_copy(
+            squares.at[blk], squares.at[blk], q_s.at[k - 1], q_r.at[k - 1],
+            device_id={"blk": lax.rem(blk + k, blocks)}, device_id_type=MESH)
+
+    for k in range(1, blocks):
+        q_copy(k).start()
+    for k in range(1, blocks):
+        src = lax.rem(blk - k + blocks, blocks)
+        pltpu.make_async_remote_copy(
+            squares.at[src], squares.at[src], q_s.at[k - 1], q_r.at[k - 1],
+            device_id={"blk": lax.rem(blk + k, blocks)}, device_id_type=MESH).wait_recv()
+
+    spread = squares[0]
+    for b in range(1, blocks):
+        spread = spread + squares[b]
+    inverse = lax.rsqrt(jnp.sum(spread, axis=1, keepdims=True) / full + 1e-5)
+
+    def scale(j, carry):
+        n = pl.ds(pl.multiple_of(j * nt, nt), nt)
+        norm_ref[:, n] = (acc[mine, n] * inverse * gain_ref[:, n].astype(jnp.float32)).astype(
+            jnp.bfloat16)
+        return carry
+
+    lax.fori_loop(0, tiles, scale, 0)
+
+    for c in range(CHUNKS):
+        @pl.when(blk + 1 < blocks)
+        def _():
+            up_copy(0, c, ctx_ref).wait_send()
+
+        @pl.when(blk > 0)
+        def _():
+            dn_copy(0, c, ctx_ref).wait_send()
+
+    def forwarded(n, carry):
+        t = n // CHUNKS
+        c = lax.rem(n, CHUNKS)
+
+        @pl.when(jnp.logical_and(inner, blk - 1 - t >= 0))
+        def _():
+            up_copy(t + 1, c).wait_send()
+
+        @pl.when(jnp.logical_and(inner, blk + 1 + t < blocks))
+        def _():
+            dn_copy(t + 1, c).wait_send()
+
+        return carry
+
+    lax.fori_loop(0, (blocks - 2) * CHUNKS, forwarded, 0)
+
+    def tile_sent(j, carry):
+        a_copy(j).wait_send()
+        for k in range(1, pairs):
+            b_copy(j, k).wait_send()
+        return carry
+
+    lax.fori_loop(0, tiles, tile_sent, 0)
+    for k in range(1, blocks):
+        q_copy(k).wait_send()
+
+
+def project(blocks, heads, context, w_out, residual, norm_gain):
+    rows, depth = context.shape
+    wide = w_out.shape[1]
+    own_rows = residual.shape[0]
+    nt = min(TILE, wide)
+    tiles = wide // nt
+    pairs = heads // 2
+    hops = (blocks - 1) * CHUNKS
+    cross = max(tiles * (pairs - 1), 1)
+    dma = pltpu.SemaphoreType.DMA
+    vmem = pl.BlockSpec(memory_space=pltpu.VMEM)
+    shape = jax.ShapeDtypeStruct((own_rows, wide), jnp.bfloat16)
+    return pl.pallas_call(
+        functools.partial(project_kernel, blocks, heads),
+        out_shape=(shape, shape),
+        in_specs=[vmem, pl.BlockSpec(memory_space=pl.ANY), vmem, vmem],
+        out_specs=(vmem, vmem),
+        scratch_shapes=[
+            pltpu.VMEM((blocks, rows, depth), jnp.bfloat16),
+            pltpu.VMEM((depth, wide), jnp.bfloat16),
+            pltpu.VMEM((blocks * rows, wide), jnp.float32),
+            pltpu.VMEM((tiles, pairs, own_rows, nt), jnp.bfloat16),
+            pltpu.VMEM((tiles, pairs, own_rows, nt), jnp.bfloat16),
+            pltpu.VMEM((cross, own_rows, nt), jnp.bfloat16),
+            pltpu.VMEM((cross, own_rows, nt), jnp.bfloat16),
+            pltpu.VMEM((blocks, own_rows, 128), jnp.float32),
+            dma((CHUNKS,)),
+            dma((hops,)), dma((hops,)), dma((hops,)), dma((hops,)),
+            dma((tiles,)), dma((tiles,)),
+            dma((cross,)), dma((cross,)),
+            dma((blocks - 1,)), dma((blocks - 1,)),
+        ],
+        compiler_params=pltpu.CompilerParams(
+            collective_id=0, has_side_effects=True, vmem_limit_bytes=56 * 2**20),
+        cost_estimate=pl.CostEstimate(
+            flops=2 * blocks * rows * depth * wide, bytes_accessed=2 * depth * wide,
+            transcendentals=0),
+        name="project",
+    )(context, w_out, residual, norm_gain.reshape(1, wide))
+
+
+def local(blocks, heads, queries, kv_cache, draft_kv, cache_len, accepted, w_out, residual,
+          norm_gain):
     seq_count = kv_cache.shape[0]
     kv_local = kv_cache.shape[2]
     head_dim = kv_cache.shape[3] // 2
@@ -52,23 +365,12 @@
     query_rows = queries.reshape(seq_count, draft_len, kv_local, group_size, head_dim)
     context = jax.vmap(attend_local)(query_rows, kv_cache, draft_kv, cache_len, accepted)
     context = context.reshape(seq_count * draft_len, -1)
-    partial_terms = jnp.dot(
-        lax.all_gather(context, "blk", axis=0, tiled=True),
-        w_out,
-        preferred_element_type=jnp.float32,
-    )
-    attended = lax.psum_scatter(partial_terms, "head", scatter_dimension=0, tiled=True)
-    summed = residual.astype(jnp.float32) + attended
-    squares = lax.psum(jnp.sum(summed * summed, axis=1), "blk")
-    full_width = summed.shape[1] * lax.axis_size("blk")
-    inverse_rms = lax.rsqrt(squares / full_width + 1e-05)
-    normed = summed * inverse_rms[:, None] * norm_gain.astype(jnp.float32)[None, :]
-    return (summed.astype(jnp.bfloat16), normed.astype(jnp.bfloat16))
+    return project(blocks, heads, context, w_out, residual, norm_gain)
 
 
 def solution(mesh):
     return jax.shard_map(
-        local,
+        functools.partial(local, mesh.shape["blk"], mesh.shape["head"]),
         mesh=mesh,
         in_specs=(
             P(("grp", "blk"), "head"),

time: 119 us -> 59.4 us (0.50)
  waiting for transfers between devices: 61.2 us -> 0 us
  Pallas kernels: 0 us -> 43.1 us
  matrix products: 19.6 us -> 2.97 us
  between operations: 14.1 us -> 0.77 us
  blocking collectives: 11.7 us -> 0 us
  local copies, waits for them, and re-layouts: 7.41 us -> 10.7 us
  other arithmetic: 4.73 us -> 1.61 us
    pallas_call x0 -> x1, Pallas kernels: none -> 43.1 us  [project(): pl.pallas_call(functools.partial(project_kernel, blocks, heads), out_shap...]
    all_gather x1 -> x0, waiting for transfers between devices: 30.7 us -> none  [local(): lax.all_gather(context, 'blk', axis=0, tiled=True)]
    reduce_scatter x1 -> x0, waiting for transfers between devices: 30.4 us -> none  [local(): lax.psum_scatter(partial_terms, 'head', scatter_dimension=0, tiled=True)]
    dot_general x1 -> x0, matrix products: 16.7 us -> none  [local(): jnp.dot(lax.all_gather(context, 'blk', axis=0, tiled=True), w_out, prefer...]
    psum x1 -> x0, blocking collectives: 11.7 us -> none  [local(): squares = lax.psum(jnp.sum(summed * summed, axis=1), 'blk')]
    unnamed x13, local copies, waits for them, and re-layouts: 0.73 us -> 3.41 us
    convert_element_type x2 -> x0, other arithmetic: 1.89 us -> none  [the longest x1 1.89 us: local(): return (summed.astype(jnp.bfloat16), normed.astype(jnp.bfloat16))]
    reduce_sum x1 -> x0, other arithmetic: 1.22 us -> none  [local(): squares = lax.psum(jnp.sum(summed * summed, axis=1), 'blk')]
  transfers between devices with their start and end apart: 2 -> 0, of which waited for: 2 -> 0; matrix products, arithmetic and copies ran while one was open for 0% -> 0% of each run, Pallas kernels for 0% -> 0%
where the time goes in v1:
time: 59.4 us; the launch traced here: 59.1 us
  Pallas kernels  43.1 us (73%)
  local copies, waits for them, and re-layouts  10.7 us (18%)
  matrix products  2.97 us (5%)
  other arithmetic  1.61 us (3%)
  between operations  0.77 us (1%)
    pallas_call x1, Pallas kernels, project(): pl.pallas_call(functools.partial(project_kernel, blocks, heads), out_shap...  43.1 us
    slice x1, local copies, waits for them, and re-layouts, attend_local(): cache_values = cache_rows[..., head_dim:]  5.72 us
    unnamed x13, local copies, waits for them, and re-layouts  3.41 us

profile of v1, /device:TPU:0, one launch (start us, length us, event | category | flops | bytes accessed | tf_op | source)
XLA Modules:
  0.0 59.1 jit_solution(5000759186532943651)
XLA Ops:
  0.6 0.7 %iota_compare_fusion = pred[8,512]{1,0:T(8,128)(4,1)S(1)} fusion(s32[8]{0:T(128)} %param.11), kind=kLoop, calls=%fused_computation.29 | loop fusion | flops 4096 | bytes 4128 | tf_op jit(solution)/shard_map/vmap()/lt | solution.py:31
  1.4 0.0 copy-start.1
  1.4 5.7 %fusion.21 = (bf16[8,512,2,128]{3,2,1,0:T(2,128)(2,1)}, bf16[8,512,2,128]{3,2,1,0:T(2,128)(2,1)S(1)}) fusion(bf16[8,512,2,256]{3,2,1,0:T(2,128)(2,1)} %param.9), kind=kLoop, calls=%fused_computation.36 | loop fusion | bytes 8388608 | tf_op jit(solution)/shard_map/vmap()/slice | solution.py:19
  7.1 0.0 copy-done.1
  7.1 0.0 copy-start.4
  7.1 0.0 copy-start.2
  7.2 1.0 %fusion.2 = (f32[8,2,4,16]{3,2,1,0:T(4,128)S(1)}, f32[8,2,4,16,512]{4,3,2,1,0:T(8,128)S(1)}) fusion(pred[8,512]{1,0:T(8,128)(4,1)S(1)} %iota_compare_fusion, bf16[8,512,2,128]{3,2,1,0:T(2,128)(2,1)S(1)} %get-tuple-element.3, bf16[8,4,2,16,128]{4,3,2,1,0:T(8,128)(2,1)S(1)} %bitcast.37), kind=kOutput, calls=%fused_computation.7 | convolution fusion | flops 135789568 | bytes 4464640 | tf_op jit(solution)/shard_map/vmap(jkgd,pkd->kjgp)/dot_general | solution.py:23
  8.1 0.0 copy-done.4
  8.2 0.1 copy.12
  8.3 0.0 copy-done.2
  8.3 0.0 copy-start
  8.3 0.8 %fusion.23 = (f32[8,2,4,16]{3,2,1,0:T(4,128)S(1)}, f32[8,2,4,16,4]{3,4,2,1,0:T(4,128)S(1)}) fusion(bf16[8,4,2,128]{3,2,1,0:T(2,128)(2,1)S(1)} %get-tuple-element.5, bf16[8,4,2,16,128]{4,3,2,1,0:T(8,128)(2,1)S(1)} %bitcast.38, pred[8,4,4]{2,1,0:T(4,128)(4,1)S(1)} %and_or_fusion), kind=kOutput, calls=%fused_computation.38 | convolution fusion | flops 1059840 | bytes 299136 | tf_op jit(solution)/shard_map/vmap(jkgd,ikd->kjgi)/dot_general | solution.py:27
  9.1 0.7 %fusion.3 = f32[8,2,4,16]{3,2,1,0:T(4,128)S(1)} fusion(f32[8,2,4,16,512]{4,3,2,1,0:T(8,128)S(1)} %get-tuple-element.7, f32[8,2,4,16]{3,2,1,0:T(4,128)S(1)} %max.7, pred[8,512]{1,0:T(8,128)(4,1)S(1)} %iota_compare_fusion), kind=kLoop, calls=%fused_computation.8 | loop fusion | flops 2096128 | bytes 2109440 | tf_op jit(solution)/shard_map/vmap()/reduce_sum | solution.py:42
  9.8 0.1 fusion.15
  10.0 0.3 fusion.16
  10.2 0.0 copy-done
  10.3 0.0 copy-start.3
  10.3 1.0 %fusion.6 = bf16[8,4,2,16,128]{4,3,1,2,0:T(8,128)(2,1)S(1)} fusion(f32[8,2,4,16,128]{4,3,2,1,0:T(8,128)S(1)} %fusion.16, bf16[8,512,2,128]{3,2,1,0:T(2,128)(2,1)S(1)} %copy-done, f32[8,2,4,16,512]{4,3,2,1,0:T(8,128)S(1)} %get-tuple-element.7, f32[8,2,4,16]{3,2,1,0:T(4,128)S(1)} %add.12, f32[8,2,4,16]{3,2,1,0:T(4,128)S(1)} %max.7, ...), kind=kOutput, calls=%fused_computation.11 | convolution fusion | flops 137101312 | bytes 4993024 | tf_op jit(solution)/shard_map/vmap(kjgp,pkd->jkgd)/dot_general | solution.py:45
  11.3 0.8 %reshape.54.ctx_ref = bf16[32,4096]{1,0:T(8,128)(2,1)} reshape(bf16[8,4,2,16,128]{4,3,2,1,0:T(8,128)(2,1)S(1)} %copy.17) | data formatting | bytes 524288 | tf_op jit(solution)/shard_map/reshape;vmap()/reshape | solution.py:367
  12.1 0.0 copy-done.3
  12.1 0.6 %reshape.55.gain_ref = bf16[1,4096]{1,0:T(2,128)(2,1)} reshape(bf16[4096]{0:T(1024)(128)(2,1)S(1)} %copy-done.3) | data formatting | bytes 16384 | tf_op jit(solution)/shard_map/reshape | solution.py:355
  12.7 43.1 %project.1 = (bf16[32,4096]{1,0:T(8,128)(2,1)}, bf16[32,4096]{1,0:T(8,128)(2,1)}) custom-call(bf16[32,4096]{1,0:T(8,128)(2,1)} %reshape.54.ctx_ref, bf16[4096,4096]{1,0:T(8,128)(2,1)} %w_ref.1, bf16[32,4096]{1,0:T(8,128)(2,1)} %res_ref.1, bf16[1,4096]{1,0:T(2,128)(2,1)} %reshape.55.gain_ref), custom_call_target="tpu_custom_call" | custom-call | flops 4294967296 | bytes 33554432 | tf_op jit(solution)/shard_map/project/pallas_call | solution.py:329
  55.8 1.7 %copy.55 = bf16[32,4096]{1,0:T(8,128)(2,1)} copy(bf16[32,4096]{1,0:T(8,128)(2,1)} %get-tuple-element.14) | data formatting | bytes 524288
  57.4 1.7 %copy.56 = bf16[32,4096]{1,0:T(8,128)(2,1)} copy(bf16[32,4096]{1,0:T(8,128)(2,1)} %get-tuple-element.15) | data formatting | bytes 524288
  (8 shorter events, 0.1 us)
Async XLA Ops:
  1.4 5.7 %copy-start.1 = (bf16[32,4096]{1,0:T(8,128)(2,1)S(1)}, bf16[32,4096]{1,0:T(8,128)(2,1)}, u32[]{:S(2)}) copy-start(bf16[32,4096]{1,0:T(8,128)(2,1)} %param.8) | copy-start | bytes 786436
  7.1 1.0 %copy-start.4 = (s32[8,4]{0,1:T(4,128)S(1)}, s32[8,4]{0,1:T(4,128)}, u32[]{:S(2)}) copy-start(s32[8,4]{0,1:T(4,128)} %param.12) | copy-start | bytes 388
  7.1 1.1 %copy-start.2 = (bf16[8,4,2,256]{3,2,1,0:T(2,128)(2,1)S(1)}, bf16[8,4,2,256]{3,2,1,0:T(2,128)(2,1)}, u32[]{:S(2)}) copy-start(bf16[8,4,2,256]{3,2,1,0:T(2,128)(2,1)} %param.10) | copy-start | bytes 98308
  8.3 1.9 %copy-start = (bf16[8,512,2,128]{3,2,1,0:T(2,128)(2,1)S(1)}, bf16[8,512,2,128]{3,2,1,0:T(2,128)(2,1)}, u32[]{:S(2)}) copy-start(bf16[8,512,2,128]{3,2,1,0:T(2,128)(2,1)} %get-tuple-element.2) | copy-start | bytes 6291460
  10.3 1.8 %copy-start.3 = (bf16[4096]{0:T(1024)(128)(2,1)S(1)}, bf16[4096]{0:T(1024)(128)(2,1)}, u32[]{:S(2)}) copy-start(bf16[4096]{0:T(1024)(128)(2,1)} %param.15) | copy-start | bytes 24580

commit v2 on v1

--- a/solution.py
+++ b/solution.py
@@ -9,55 +9,95 @@
 
 MESH = pl.DeviceIdType.MESH
 CHUNKS = 4
-TILE = 512
-
-
-def attend_local(query_rows, cache_rows, draft_rows, length, accept_row):
-    head_dim = cache_rows.shape[-1] // 2
-    scaling = head_dim ** (-0.5)
-    cache_keys = cache_rows[..., :head_dim]
-    cache_values = cache_rows[..., head_dim:]
-    draft_keys = draft_rows[..., :head_dim]
-    draft_values = draft_rows[..., head_dim:]
-    cache_scores = (
-        jnp.einsum("jkgd,pkd->kjgp", query_rows, cache_keys, preferred_element_type=jnp.float32)
-        * scaling
-    )
-    draft_scores = (
-        jnp.einsum("jkgd,ikd->kjgi", query_rows, draft_keys, preferred_element_type=jnp.float32)
-        * scaling
-    )
-    slots = jnp.arange(cache_rows.shape[0], dtype=jnp.int32)
-    cache_scores = jnp.where(slots < length, cache_scores, -1e30)
-    draft_len = draft_rows.shape[0]
-    later = jnp.arange(draft_len, dtype=jnp.int32)[:, None]
-    earlier = jnp.arange(draft_len, dtype=jnp.int32)[None, :]
-    visible = (earlier == later) | (earlier < later) & (accept_row[None, :] == 1)
-    draft_scores = jnp.where(visible[None, :, None, :], draft_scores, -1e30)
-    top_score = jnp.maximum(jnp.max(cache_scores, axis=-1), jnp.max(draft_scores, axis=-1))[
-        ..., None
-    ]
-    cache_exp = jnp.exp(cache_scores - top_score)
-    draft_exp = jnp.exp(draft_scores - top_score)
-    totals = jnp.sum(cache_exp, axis=-1, keepdims=True) + jnp.sum(draft_exp, axis=-1, keepdims=True)
-    cache_probs = (cache_exp / totals).astype(jnp.bfloat16)
-    draft_probs = (draft_exp / totals).astype(jnp.bfloat16)
-    context = jnp.einsum(
-        "kjgp,pkd->jkgd", cache_probs, cache_values, preferred_element_type=jnp.float32
-    )
-    context = context + jnp.einsum(
-        "kjgi,ikd->jkgd", draft_probs, draft_values, preferred_element_type=jnp.float32
-    )
-    return context.astype(jnp.bfloat16).reshape(draft_len, -1)
+TILE = 1024
+
+
+def attention(scr, q_ref, kv_ref, draft_ref, len_ref, acc_ref, gat, blk):
+    keys, vals, qf, qs, cf, k_sem, v_sem = scr
+    seqs, slots, kvh, two = kv_ref.shape
+    hd = two // 2
+    drafts = draft_ref.shape[1]
+    heads = q_ref.shape[1] // hd
+    group = heads // kvh
+    n = group * drafts
+    cols = slots * kvh
+    scaling = hd ** (-0.5)
+    over_last = (((1,), (1,)), ((), ()))
+
+    def copies(s):
+        return (
+            pltpu.make_async_copy(kv_ref.at[s, :, :, pl.ds(0, hd)], keys.at[s], k_sem.at[s]),
+            pltpu.make_async_copy(kv_ref.at[s, :, :, pl.ds(hd, hd)], vals.at[s], v_sem.at[s]),
+        )
+
+    def load():
+        for s in range(seqs):
+            for copy in copies(s):
+                copy.start()
+
+    def prepare():
+        qf[...] = q_ref[...].astype(jnp.float32)
+        for s in range(seqs):
+            for h in range(heads):
+                qs[s, h * drafts:(h + 1) * drafts, :] = (
+                    qf[s * drafts:(s + 1) * drafts, h * hd:(h + 1) * hd])
+
+    def one_head(kh):
+        col = lax.broadcasted_iota(jnp.int32, (n, cols), 1)
+        slot = jnp.where(col % kvh == kh, col // kvh, 2**30)
+        shape = (n, drafts * kvh)
+        j = lax.broadcasted_iota(jnp.int32, shape, 0) % drafts
+        dcol = lax.broadcasted_iota(jnp.int32, shape, 1)
+        i = dcol // kvh
+        mine = dcol % kvh == kh
+        for s in range(seqs):
+            if kh == 0:
+                for copy in copies(s):
+                    copy.wait()
+            q = qs[s, kh * n:(kh + 1) * n, :].astype(jnp.bfloat16)
+            k = keys[s].reshape(cols, hd)
+            v = vals[s].reshape(cols, hd)
+            d = draft_ref[s].astype(jnp.float32).reshape(drafts * kvh, two).astype(jnp.bfloat16)
+            scores = lax.dot_general(
+                q, k, over_last, preferred_element_type=jnp.float32) * scaling
+            scores = jnp.where(slot < len_ref[s], scores, -1e30)
+            draft_scores = lax.dot_general(
+                q, d[:, :hd], over_last, preferred_element_type=jnp.float32) * scaling
+            taken = jnp.zeros(shape, jnp.int32)
+            for x in range(drafts):
+                taken = jnp.where(i == x, acc_ref[s, x], taken)
+            visible = mine & ((i == j) | ((i < j) & (taken == 1)))
+            draft_scores = jnp.where(visible, draft_scores, -1e30)
+            top = jnp.maximum(jnp.max(scores, axis=1, keepdims=True),
+                              jnp.max(draft_scores, axis=1, keepdims=True))
+            e = jnp.exp(scores - top)
+            de = jnp.exp(draft_scores - top)
+            inverse = 1.0 / (jnp.sum(e, axis=1, keepdims=True)
+                             + jnp.sum(de, axis=1, keepdims=True))
+            out = jnp.dot((e * inverse).astype(jnp.bfloat16), v,
+                          preferred_element_type=jnp.float32)
+            out = out + jnp.dot((de * inverse).astype(jnp.bfloat16), d[:, hd:],
+                                preferred_element_type=jnp.float32)
+            for g in range(group):
+                h = kh * group + g
+                cf[s * drafts:(s + 1) * drafts, h * hd:(h + 1) * hd] = (
+                    out[g * drafts:(g + 1) * drafts, :])
+        at = slice(kh * group * hd, (kh + 1) * group * hd)
+        gat[pl.ds(blk, 1), :, at] = cf[:, at].astype(jnp.bfloat16)[None]
+
+    return load, prepare, one_head
 
 
 def project_kernel(
     blocks, heads,
-    ctx_ref, w_ref, res_ref, gain_ref, out_ref, norm_ref,
+    q_ref, kv_ref, draft_ref, len_ref, acc_ref, w_ref, res_ref, sum_ref, inv_ref,
+    keys, vals, qf, qs, cf, k_sem, v_sem,
     gat, wv, acc, send_a, recv_a, send_b, recv_b, squares,
     w_sem, up_s, up_r, dn_s, dn_r, a_s, a_r, b_s, b_r, q_s, q_r,
 ):
-    rows, depth = ctx_ref.shape
+    rows, depth = q_ref.shape
+    kvh = kv_ref.shape[2]
+    ready = CHUNKS // kvh
     wide = w_ref.shape[1]
     own_rows = res_ref.shape[0]
     kc = depth // CHUNKS
@@ -75,19 +115,19 @@
         part = pl.ds(c * kc, kc)
         return pltpu.make_async_copy(w_ref.at[part], wv.at[part], w_sem.at[c])
 
-    def up_copy(t, c, src=None):
+    def up_copy(t, c):
         block = lax.rem(blk - t + blocks, blocks)
         cols = pl.ds(pl.multiple_of(c * kc, kc), kc)
-        src = gat.at[block, :, cols] if src is None else src.at[:, cols]
+        src = gat.at[block, :, cols]
         n = t * CHUNKS + c
         return pltpu.make_async_remote_copy(
             src, gat.at[block, :, cols], up_s.at[n], up_r.at[n],
             device_id={"blk": lax.rem(blk + 1, blocks)}, device_id_type=MESH)
 
-    def dn_copy(t, c, src=None):
+    def dn_copy(t, c):
         block = lax.rem(blk + t, blocks)
         cols = pl.ds(pl.multiple_of(c * kc, kc), kc)
-        src = gat.at[block, :, cols] if src is None else src.at[:, cols]
+        src = gat.at[block, :, cols]
         n = t * CHUNKS + c
         return pltpu.make_async_remote_copy(
             src, gat.at[block, :, cols], dn_s.at[n], dn_r.at[n],
@@ -109,6 +149,10 @@
             gat.at[block, :, cols], gat.at[block, :, cols], dn_s.at[n], dn_r.at[n],
             device_id={"blk": lax.rem(blk + 1, blocks)}, device_id_type=MESH).wait_recv()
 
+    load, prepare, one_head = attention(
+        (keys, vals, qf, qs, cf, k_sem, v_sem),
+        q_ref, kv_ref, draft_ref, len_ref, acc_ref, gat, blk)
+    load()
     for c in range(CHUNKS):
         w_copy(c).start()
 
@@ -121,38 +165,42 @@
         pl.semaphore_signal(
             barrier, inc=1,
             device_id={"head": lax.rem(chip + k, pairs) * 2 + side}, device_id_type=MESH)
+    prepare()
+    one_head(0)
     pl.semaphore_wait(barrier, blocks - 1 + 1 + pairs - 1)
 
-    for c in range(CHUNKS):
+    inner = jnp.logical_and(blk > 0, blk + 1 < blocks)
+
+    def send_own(c):
         @pl.when(blk + 1 < blocks)
         def _():
-            up_copy(0, c, ctx_ref).start()
+            up_copy(0, c).start()
 
         @pl.when(blk > 0)
         def _():
-            dn_copy(0, c, ctx_ref).start()
-
-    gat[pl.ds(blk, 1)] = ctx_ref[...][None]
-
-    inner = jnp.logical_and(blk > 0, blk + 1 < blocks)
-
-    def forward(n, carry):
-        t = n // CHUNKS
-        c = lax.rem(n, CHUNKS)
-
-        @pl.when(jnp.logical_and(inner, blk - 1 - t >= 0))
-        def _():
-            up_wait(t, c)
-            up_copy(t + 1, c).start()
-
-        @pl.when(jnp.logical_and(inner, blk + 1 + t < blocks))
-        def _():
-            dn_wait(t, c)
-            dn_copy(t + 1, c).start()
-
-        return carry
-
-    lax.fori_loop(0, (blocks - 2) * CHUNKS, forward, 0)
+            dn_copy(0, c).start()
+
+    def forward(c):
+        def one(t, carry):
+            @pl.when(jnp.logical_and(inner, blk - 1 - t >= 0))
+            def _():
+                up_wait(t, c)
+                up_copy(t + 1, c).start()
+
+            @pl.when(jnp.logical_and(inner, blk + 1 + t < blocks))
+            def _():
+                dn_wait(t, c)
+                dn_copy(t + 1, c).start()
+
+            return carry
+
+        lax.fori_loop(0, blocks - 2, one, 0)
+
+    ahead = min(2, ready)
+    for c in range(ahead):
+        send_own(c)
+    for kh in range(1, kvh):
+        one_head(kh)
 
     def arrived(c):
         w_copy(c).wait()
@@ -174,9 +222,7 @@
         x = gat[:, :, c * kc:(c + 1) * kc].reshape(blocks * rows, kc)
         return jnp.dot(x, wv[c * kc:(c + 1) * kc, n], preferred_element_type=jnp.float32)
 
-    for c in range(CHUNKS - 1):
-        arrived(c)
-
+    def add_chunk(c):
         def tile_of(j, carry):
             n = pl.ds(pl.multiple_of(j * nt, nt), nt)
             if c == 0:
@@ -186,6 +232,14 @@
             return carry
 
         lax.fori_loop(0, tiles, tile_of, 0)
+
+    for c in range(CHUNKS):
+        forward(c)
+        if c + ahead < CHUNKS:
+            send_own(c + ahead)
+        if c > 0:
+            arrived(c - 1)
+            add_chunk(c - 1)
 
     arrived(CHUNKS - 1)
 
@@ -241,8 +295,7 @@
             b_copy(j, k).wait_recv()
             total = total + recv_b[j * (pairs - 1) + k - 1].astype(jnp.float32)
         total = total + res_ref[:, n].astype(jnp.float32)
-        acc[mine, n] = total
-        out_ref[:, n] = total.astype(jnp.bfloat16)
+        sum_ref[:, n] = total
         power = total * total
         part = power[:, 0:128]
         for v in range(1, nt // 128):
@@ -269,23 +322,16 @@
     for b in range(1, blocks):
         spread = spread + squares[b]
     inverse = lax.rsqrt(jnp.sum(spread, axis=1, keepdims=True) / full + 1e-5)
-
-    def scale(j, carry):
-        n = pl.ds(pl.multiple_of(j * nt, nt), nt)
-        norm_ref[:, n] = (acc[mine, n] * inverse * gain_ref[:, n].astype(jnp.float32)).astype(
-            jnp.bfloat16)
-        return carry
-
-    lax.fori_loop(0, tiles, scale, 0)
+    inv_ref[...] = jnp.broadcast_to(inverse, inv_ref.shape)
 
     for c in range(CHUNKS):
         @pl.when(blk + 1 < blocks)
         def _():
-            up_copy(0, c, ctx_ref).wait_send()
+            up_copy(0, c).wait_send()
 
         @pl.when(blk > 0)
         def _():
-            dn_copy(0, c, ctx_ref).wait_send()
+            dn_copy(0, c).wait_send()
 
     def forwarded(n, carry):
         t = n // CHUNKS
@@ -314,8 +360,12 @@
         q_copy(k).wait_send()
 
 
-def project(blocks, heads, context, w_out, residual, norm_gain):
-    rows, depth = context.shape
+def local(blocks, heads, queries, kv_cache, draft_kv, cache_len, accepted, w_out, residual,
+          norm_gain):
+    rows, depth = queries.shape
+    seqs, slots, kvh, two = kv_cache.shape
+    hd = two // 2
+    drafts = draft_kv.shape[1]
     wide = w_out.shape[1]
     own_rows = residual.shape[0]
     nt = min(TILE, wide)
@@ -325,13 +375,23 @@
     cross = max(tiles * (pairs - 1), 1)
     dma = pltpu.SemaphoreType.DMA
     vmem = pl.BlockSpec(memory_space=pltpu.VMEM)
-    shape = jax.ShapeDtypeStruct((own_rows, wide), jnp.bfloat16)
-    return pl.pallas_call(
+    smem = pl.BlockSpec(memory_space=pltpu.SMEM)
+    anywhere = pl.BlockSpec(memory_space=pl.ANY)
+    summed, inverse = pl.pallas_call(
         functools.partial(project_kernel, blocks, heads),
-        out_shape=(shape, shape),
-        in_specs=[vmem, pl.BlockSpec(memory_space=pl.ANY), vmem, vmem],
+        out_shape=(
+            jax.ShapeDtypeStruct((own_rows, wide), jnp.float32),
+            jax.ShapeDtypeStruct((own_rows, 128), jnp.float32),
+        ),
+        in_specs=[vmem, anywhere, vmem, smem, smem, anywhere, vmem],
         out_specs=(vmem, vmem),
         scratch_shapes=[
+            pltpu.VMEM((seqs, slots, kvh, hd), jnp.bfloat16),
+            pltpu.VMEM((seqs, slots, kvh, hd), jnp.bfloat16),
+            pltpu.VMEM((rows, depth), jnp.float32),
+            pltpu.VMEM((seqs, depth // hd * drafts, hd), jnp.float32),
+            pltpu.VMEM((rows, depth), jnp.float32),
+            dma((seqs,)), dma((seqs,)),
             pltpu.VMEM((blocks, rows, depth), jnp.bfloat16),
             pltpu.VMEM((depth, wide), jnp.bfloat16),
             pltpu.VMEM((blocks * rows, wide), jnp.float32),
@@ -352,20 +412,9 @@
             flops=2 * blocks * rows * depth * wide, bytes_accessed=2 * depth * wide,
             transcendentals=0),
         name="project",
-    )(context, w_out, residual, norm_gain.reshape(1, wide))
-
-
-def local(blocks, heads, queries, kv_cache, draft_kv, cache_len, accepted, w_out, residual,
-          norm_gain):
-    seq_count = kv_cache.shape[0]
-    kv_local = kv_cache.shape[2]
-    head_dim = kv_cache.shape[3] // 2
-    draft_len = draft_kv.shape[1]
-    group_size = queries.shape[1] // (kv_local * head_dim)
-    query_rows = queries.reshape(seq_count, draft_len, kv_local, group_size, head_dim)
-    context = jax.vmap(attend_local)(query_rows, kv_cache, draft_kv, cache_len, accepted)
-    context = context.reshape(seq_count * draft_len, -1)
-    return project(blocks, heads, context, w_out, residual, norm_gain)
+    )(queries, kv_cache, draft_kv, cache_len, accepted, w_out, residual)
+    normed = summed * inverse[:, :1] * norm_gain.astype(jnp.float32)[None, :]
+    return (summed.astype(jnp.bfloat16), normed.astype(jnp.bfloat16))
 
 
 def solution(mesh):

time: 59.4 us -> 60.7 us (1.022)
  Pallas kernels: 43.1 us -> 54.8 us
  local copies, waits for them, and re-layouts: 10.7 us -> 2.18 us
  matrix products: 2.97 us -> 0 us
  other arithmetic: 1.61 us -> 2.73 us
    pallas_call x1, Pallas kernels: 43.1 us -> 54.8 us  [local(): pl.pallas_call(functools.partial(project_kernel, blocks, heads), out_shap...]
    slice x2 -> x1, local copies, waits for them, and re-layouts: 5.74 us -> 0.83 us  [local(): normed = summed * inverse[:, :1] * norm_gain.astype(jnp.float32)[None, :]]
    dot_general x4 -> x0, matrix products: 2.97 us -> none  [the longest x1 0.98 us: attend_local(): jnp.einsum('jkgd,pkd->kjgp', query_rows, cache_keys, preferred_element_ty...]
    convert_element_type x0 -> x2, other arithmetic: none -> 2.73 us  [the longest x1 2.03 us: local(): return (summed.astype(jnp.bfloat16), normed.astype(jnp.bfloat16))]
    unnamed x13 -> x1, local copies, waits for them, and re-layouts: 3.41 us -> 1.35 us
    reshape x2 -> x0, local copies, waits for them, and re-layouts: 1.43 us -> none  [the longest x1 0.82 us: local(): context = context.reshape(seq_count * draft_len, -1)]
    reduce_sum x2 -> x0, other arithmetic: 0.83 us -> none  [the longest x1 0.69 us: attend_local(): jnp.sum(cache_exp, axis=-1, keepdims=True)]
    lt x2 -> x0, other arithmetic: 0.74 us -> none  [the longest x1 0.73 us: attend_local(): cache_scores = jnp.where(slots < length, cache_scores, -1e+30)]
where the time goes in v2:
time: 60.7 us; the launch traced here: 60.4 us
  Pallas kernels  54.8 us (90%)
  other arithmetic  2.73 us (4%)
  local copies, waits for them, and re-layouts  2.18 us (4%)
  between operations  0.64 us (1%)
    pallas_call x1, Pallas kernels, local(): pl.pallas_call(functools.partial(project_kernel, blocks, heads), out_shap...  54.8 us
    convert_element_type x1, other arithmetic, local(): return (summed.astype(jnp.bfloat16), normed.astype(jnp.bfloat16))  2.03 us
    unnamed x1, local copies, waits for them, and re-layouts  1.35 us

profile of v2, /device:TPU:0, one launch (start us, length us, event | category | flops | bytes accessed | tf_op | source)
XLA Modules:
  0.0 60.4 jit_solution(17947419894090095040)
XLA Ops:
  0.6 1.3 %copy.11.acc_ref = s32[8,4]{1,0:T(8,128)} copy(s32[8,4]{0,1:T(4,128)} %param.12) | data formatting | bytes 256 | tf_op args[4]
  2.0 0.7 %convert_element_type.10 = f32[4096]{0:T(1024)S(1)} convert(bf16[4096]{0:T(1024)(128)(2,1)} %param.15) | non-fusion elementwise | flops 4096 | bytes 24576 | tf_op jit(solution)/shard_map/convert_element_type | solution.py:416
  2.7 54.8 %project.1 = (f32[32,4096]{1,0:T(8,128)}, f32[32,128]{1,0:T(8,128)}) custom-call(bf16[32,4096]{1,0:T(8,128)(2,1)} %q_ref.1, bf16[8,512,2,256]{3,2,1,0:T(2,128)(2,1)} %kv_ref.1, bf16[8,4,2,256]{3,2,1,0:T(2,128)(2,1)} %draft_ref.1, s32[8]{0:T(128)} %len_ref.1, s32[8,4]{1,0:T(8,128)} %copy.11.acc_ref, bf16[4096,4096]{1,0:T(8,128)(2,1)} %w_ref.1, ...), custom_call_target="tpu_custom_call" | custom-call | flops 4294967296 | bytes 33554432 | tf_op jit(solution)/shard_map/project/pallas_call | solution.py:380
  57.5 0.8 %slice_reduce_fusion = f32[32]{0:T(128)S(1)} fusion(f32[32,128]{1,0:T(8,128)} %get-tuple-element.5), kind=kLoop, calls=%fused_computation.1 | loop fusion | bytes 256 | tf_op jit(solution)/shard_map/slice | solution.py:416
  58.4 2.0 %multiply_convert_fusion = (bf16[32,4096]{1,0:T(8,128)(2,1)}, bf16[32,4096]{1,0:T(8,128)(2,1)}) fusion(f32[32,4096]{1,0:T(8,128)} %get-tuple-element.4, f32[4096]{0:T(1024)S(1)} %convert_element_type.10, f32[32]{0:T(128)S(1)} %slice_reduce_fusion), kind=kLoop, calls=%fused_computation | loop fusion | flops 524288 | bytes 1065088 | tf_op jit(solution)/shard_map/convert_element_type | solution.py:417

commit v3 on v2

--- a/solution.py
+++ b/solution.py
@@ -8,12 +8,12 @@
 from jax.sharding import PartitionSpec as P
 
 MESH = pl.DeviceIdType.MESH
-CHUNKS = 4
+CHUNKS = 2
 TILE = 1024
 
 
 def attention(scr, q_ref, kv_ref, draft_ref, len_ref, acc_ref, gat, blk):
-    keys, vals, qf, qs, cf, k_sem, v_sem = scr
+    cache, qf, qs, cf, kv_sem = scr
     seqs, slots, kvh, two = kv_ref.shape
     hd = two // 2
     drafts = draft_ref.shape[1]
@@ -25,15 +25,11 @@
     over_last = (((1,), (1,)), ((), ()))
 
     def copies(s):
-        return (
-            pltpu.make_async_copy(kv_ref.at[s, :, :, pl.ds(0, hd)], keys.at[s], k_sem.at[s]),
-            pltpu.make_async_copy(kv_ref.at[s, :, :, pl.ds(hd, hd)], vals.at[s], v_sem.at[s]),
-        )
+        return pltpu.make_async_copy(kv_ref.at[s], cache.at[s], kv_sem.at[s])
 
     def load():
         for s in range(seqs):
-            for copy in copies(s):
-                copy.start()
+            copies(s).start()
 
     def prepare():
         qf[...] = q_ref[...].astype(jnp.float32)
@@ -52,11 +48,10 @@
         mine = dcol % kvh == kh
         for s in range(seqs):
             if kh == 0:
-                for copy in copies(s):
-                    copy.wait()
+                copies(s).wait()
             q = qs[s, kh * n:(kh + 1) * n, :].astype(jnp.bfloat16)
-            k = keys[s].reshape(cols, hd)
-            v = vals[s].reshape(cols, hd)
+            k = cache[s, :, :, :hd].reshape(cols, hd)
+            v = cache[s, :, :, hd:].reshape(cols, hd)
             d = draft_ref[s].astype(jnp.float32).reshape(drafts * kvh, two).astype(jnp.bfloat16)
             scores = lax.dot_general(
                 q, k, over_last, preferred_element_type=jnp.float32) * scaling
@@ -65,7 +60,7 @@
                 q, d[:, :hd], over_last, preferred_element_type=jnp.float32) * scaling
             taken = jnp.zeros(shape, jnp.int32)
             for x in range(drafts):
-                taken = jnp.where(i == x, acc_ref[s, x], taken)
+                taken = jnp.where(i == x, acc_ref[x, s], taken)
             visible = mine & ((i == j) | ((i < j) & (taken == 1)))
             draft_scores = jnp.where(visible, draft_scores, -1e30)
             top = jnp.maximum(jnp.max(scores, axis=1, keepdims=True),
@@ -91,7 +86,7 @@
 def project_kernel(
     blocks, heads,
     q_ref, kv_ref, draft_ref, len_ref, acc_ref, w_ref, res_ref, sum_ref, inv_ref,
-    keys, vals, qf, qs, cf, k_sem, v_sem,
+    cache, qf, qs, cf, kv_sem,
     gat, wv, acc, send_a, recv_a, send_b, recv_b, squares,
     w_sem, up_s, up_r, dn_s, dn_r, a_s, a_r, b_s, b_r, q_s, q_r,
 ):
@@ -150,7 +145,7 @@
             device_id={"blk": lax.rem(blk + 1, blocks)}, device_id_type=MESH).wait_recv()
 
     load, prepare, one_head = attention(
-        (keys, vals, qf, qs, cf, k_sem, v_sem),
+        (cache, qf, qs, cf, kv_sem),
         q_ref, kv_ref, draft_ref, len_ref, acc_ref, gat, blk)
     load()
     for c in range(CHUNKS):
@@ -196,11 +191,13 @@
 
         lax.fori_loop(0, blocks - 2, one, 0)
 
-    ahead = min(2, ready)
-    for c in range(ahead):
-        send_own(c)
-    for kh in range(1, kvh):
-        one_head(kh)
+    for kh in range(kvh):
+        if kh:
+            one_head(kh)
+        for c in range(kh * ready, (kh + 1) * ready):
+            send_own(c)
+    for c in range(CHUNKS):
+        forward(c)
 
     def arrived(c):
         w_copy(c).wait()
@@ -233,13 +230,9 @@
 
         lax.fori_loop(0, tiles, tile_of, 0)
 
-    for c in range(CHUNKS):
-        forward(c)
-        if c + ahead < CHUNKS:
-            send_own(c + ahead)
-        if c > 0:
-            arrived(c - 1)
-            add_chunk(c - 1)
+    for c in range(CHUNKS - 1):
+        arrived(c)
+        add_chunk(c)
 
     arrived(CHUNKS - 1)
 
@@ -322,7 +315,7 @@
     for b in range(1, blocks):
         spread = spread + squares[b]
     inverse = lax.rsqrt(jnp.sum(spread, axis=1, keepdims=True) / full + 1e-5)
-    inv_ref[...] = jnp.broadcast_to(inverse, inv_ref.shape)
+    inv_ref[...] = inverse
 
     for c in range(CHUNKS):
         @pl.when(blk + 1 < blocks)
@@ -381,17 +374,16 @@
         functools.partial(project_kernel, blocks, heads),
         out_shape=(
             jax.ShapeDtypeStruct((own_rows, wide), jnp.float32),
-            jax.ShapeDtypeStruct((own_rows, 128), jnp.float32),
+            jax.ShapeDtypeStruct((own_rows, 1), jnp.float32),
         ),
         in_specs=[vmem, anywhere, vmem, smem, smem, anywhere, vmem],
         out_specs=(vmem, vmem),
         scratch_shapes=[
-            pltpu.VMEM((seqs, slots, kvh, hd), jnp.bfloat16),
-            pltpu.VMEM((seqs, slots, kvh, hd), jnp.bfloat16),
+            pltpu.VMEM((seqs, slots, kvh, two), jnp.bfloat16),
             pltpu.VMEM((rows, depth), jnp.float32),
             pltpu.VMEM((seqs, depth // hd * drafts, hd), jnp.float32),
             pltpu.VMEM((rows, depth), jnp.float32),
-            dma((seqs,)), dma((seqs,)),
+            dma((seqs,)),
             pltpu.VMEM((blocks, rows, depth), jnp.bfloat16),
             pltpu.VMEM((depth, wide), jnp.bfloat16),
             pltpu.VMEM((blocks * rows, wide), jnp.float32),
@@ -412,8 +404,8 @@
             flops=2 * blocks * rows * depth * wide, bytes_accessed=2 * depth * wide,
             transcendentals=0),
         name="project",
-    )(queries, kv_cache, draft_kv, cache_len, accepted, w_out, residual)
-    normed = summed * inverse[:, :1] * norm_gain.astype(jnp.float32)[None, :]
+    )(queries, kv_cache, draft_kv, cache_len, accepted.T, w_out, residual)
+    normed = summed * inverse * norm_gain.astype(jnp.float32)[None, :]
     return (summed.astype(jnp.bfloat16), normed.astype(jnp.bfloat16))
 
 

time: 60.7 us -> 51.4 us (0.85)
  Pallas kernels: 54.8 us -> 46.9 us
  local copies, waits for them, and re-layouts: 2.18 us -> 0 us
  other arithmetic: 2.73 us -> 3.56 us
    pallas_call x1, Pallas kernels: 54.8 us -> 46.9 us  [local(): pl.pallas_call(functools.partial(project_kernel, blocks, heads), out_shap...]
    unnamed x1 -> x0, local copies, waits for them, and re-layouts: 1.35 us -> none
    pallas_call x0 -> x1, other arithmetic: none -> 0.83 us  [local(): pl.pallas_call(functools.partial(project_kernel, blocks, heads), out_shap...]
    slice x1 -> x0, local copies, waits for them, and re-layouts: 0.83 us -> none  [local(): normed = summed * inverse[:, :1] * norm_gain.astype(jnp.float32)[None, :]]
where the time goes in v3:
time: 51.4 us; the launch traced here: 51.1 us
  Pallas kernels  46.9 us (91%)
  other arithmetic  3.56 us (7%)
  between operations  0.64 us (1%)
    pallas_call x1, Pallas kernels, local(): pl.pallas_call(functools.partial(project_kernel, blocks, heads), out_shap...  46.9 us
    convert_element_type x1, other arithmetic, local(): return (summed.astype(jnp.bfloat16), normed.astype(jnp.bfloat16))  2.02 us

profile of v3, /device:TPU:0, one launch (start us, length us, event | category | flops | bytes accessed | tf_op | source)
XLA Modules:
  0.0 51.1 jit_solution(11856563694481172969)
XLA Ops:
  0.6 0.7 %convert_element_type.10 = f32[4096]{0:T(1024)S(1)} convert(bf16[4096]{0:T(1024)(128)(2,1)} %param.15) | non-fusion elementwise | flops 4096 | bytes 24576 | tf_op jit(solution)/shard_map/convert_element_type | solution.py:408
  1.3 46.9 %project.1 = (f32[32,4096]{1,0:T(8,128)}, f32[32,1]{1,0:T(8,128)}) custom-call(bf16[32,4096]{1,0:T(8,128)(2,1)} %q_ref.1, bf16[8,512,2,256]{3,2,1,0:T(2,128)(2,1)} %kv_ref.1, bf16[8,4,2,256]{3,2,1,0:T(2,128)(2,1)} %draft_ref.1, s32[8]{0:T(128)} %len_ref.1, s32[4,8]{1,0:T(4,128)} %bitcast.1, bf16[4096,4096]{1,0:T(8,128)(2,1)} %w_ref.1, bf16[32,4096]{1,0:T(8,128)(2,1)} %res_ref.1), custom_call_target="tpu_custom_call" | custom-call | flops 4294967296 | bytes 33554432 | tf_op jit(solution)/shard_map/project/pallas_call | solution.py:373
  48.2 0.8 %reduce = f32[32]{0:T(128)S(1)} reduce(f32[32,1]{1,0:T(8,128)} %get-tuple-element.5, f32[]{:T(128)} %constant.2), dimensions={1}, to_apply=%get-tuple-element.5.reduce_sub_computation | reduce | bytes 260 | tf_op jit(solution)/shard_map/project/pallas_call | solution.py:373
  49.0 2.0 %multiply_convert_fusion = (bf16[32,4096]{1,0:T(8,128)(2,1)}, bf16[32,4096]{1,0:T(8,128)(2,1)}) fusion(f32[32,4096]{1,0:T(8,128)} %get-tuple-element.4, f32[4096]{0:T(1024)S(1)} %convert_element_type.10, f32[32]{0:T(128)S(1)} %reduce), kind=kLoop, calls=%fused_computation | loop fusion | flops 524288 | bytes 1065088 | tf_op jit(solution)/shard_map/convert_element_type | solution.py:409
